TPU v7x, 32 devices: a whole 2x2x4 slice. The times are simulated.
32 devices in a mesh: rep: 8 (over y, x, core), shard: 4 (over z).
Axes of the slice: x: 2, y: 2, z: 4, core: 2. Of those that a mesh axis runs over, the one named last changes fastest.
Arguments:
- gradients: bfloat16 [8, 96, 2560], P(None, 'shard')
- momentum: float32 [8, 96, 2560], P(None, 'shard'), may hold values from -60 to 60
Outputs:
- updates: bfloat16 [8, 96, 2560], P(None, 'shard', 'rep')
- new_momentum: float32 [8, 96, 2560], P(None, 'shard')
All inputs are finite; a program needn't handle non-finite values.
Results may differ from a plain program's by a relative error of at most 0.0014.
Values may be sent and summed in bfloat16 or wider, within the bound.
A program may use at most 64 MiB of HBM per device.

v0:
```python
import math
import jax
import jax.numpy as jnp
from jax import lax
from jax.sharding import PartitionSpec as P

E = 96
D = 2560
ITERS = 5
momentum_decay = 0.95
norm_floor = 1e-07
quintic_terms = (3.4445, -4.775, 2.0315)


def broadcast(x, axis, root):
    mine = lax.axis_index(axis) == root
    return lax.psum(jnp.where(mine, x, jnp.zeros_like(x)), axis)


def batched_schulz(effective):
    totals = jnp.sqrt(jnp.sum(effective * effective, axis=(1, 2), keepdims=True))
    iterate = effective / (totals + norm_floor)
    for turn in range(ITERS):
        gram_mat = jnp.einsum("kij,klj->kil", iterate, iterate, precision=lax.Precision.HIGHEST)
        square_mat = jnp.einsum("kij,kjl->kil", gram_mat, gram_mat, precision=lax.Precision.HIGHEST)
        poly_mat = quintic_terms[1] * gram_mat + quintic_terms[2] * square_mat
        iterate = quintic_terms[0] * iterate + jnp.einsum(
            "kij,kjl->kil", poly_mat, iterate, precision=lax.Precision.HIGHEST
        )
    return iterate


def per_device(gradients, momentum):
    update_scale = 0.2 * math.sqrt(max(E, D))
    gradient_values = gradients.astype(jnp.float32)
    new_momentum = momentum_decay * momentum + gradient_values
    effective_rows = gradient_values + momentum_decay * new_momentum
    effective = lax.all_to_all(effective_rows, "shard", split_axis=0, concat_axis=1, tiled=True)
    slot_count = effective.shape[0]
    replicas = lax.axis_size("rep")
    column = lax.axis_index("shard")
    replica = lax.axis_index("rep")
    slot_owners = (column * slot_count + jnp.arange(slot_count, dtype=jnp.int32)) % replicas
    owned = slot_owners == replica

    def compute_update(operand):
        return (update_scale * batched_schulz(operand)).astype(jnp.bfloat16)

    def skip_update(operand):
        return jnp.zeros(operand.shape, jnp.bfloat16)

    local_updates = lax.cond(jnp.any(owned), compute_update, skip_update, effective)
    copies = []
    for slot_index in range(slot_count):
        copies.append(broadcast(local_updates[slot_index], "rep", slot_owners[slot_index]))
    stacked = jnp.stack(copies)
    result_rows = lax.all_to_all(stacked, "shard", split_axis=1, concat_axis=0, tiled=True)
    col_width = result_rows.shape[2] // replicas
    kept_cols = lax.dynamic_slice_in_dim(result_rows, replica * col_width, col_width, 2)
    return (kept_cols, new_momentum)


def solution(mesh):
    in_specs = (P(None, "shard", None), P(None, "shard", None))
    out_specs = (P(None, "shard", "rep"), P(None, "shard", None))
    return jax.shard_map(
        per_device, mesh=mesh, in_specs=in_specs, out_specs=out_specs, check_vma=False
    )
```

profile of v0, /device:TPU:0, one launch (start us, length us, event | category | flops | bytes accessed | tf_op | source)
XLA Modules:
  0.0 180.7 jit_solution(16023603056860702382)
XLA Ops:
  7.2 4.4 %convert_add_fusion = (f32[8,24,2560]{2,1,0:T(8,128)}, f32[8,24,2560]{2,1,0:T(8,128)}) fusion(bf16[8,24,2560]{2,1,0:T(8,128)(2,1)} %param.4, f32[8,24,2560]{2,1,0:T(8,128)} %param.5), kind=kLoop, calls=%fused_computation.22 | loop fusion | flops 2457600 | bytes 6881280 | tf_op jit(solution)/shard_map/add | solution.py:37
  11.5 6.3 %all-to-all-start = ((f32[8,24,2560]{2,1,0:T(8,128)}), f32[8,24,2560]{2,1,0:T(8,128)S(1)}, u32[]{:S(2)}, u32[]{:S(2)}) async-start(f32[8,24,2560]{2,1,0:T(8,128)} %get-tuple-element.20), calls=%async_computation | async-start | bytes 3932160 | tf_op jit(solution)/shard_map/all_to_all | solution.py:38
  17.8 0.0 all-reduce.3.cloned.1.call-start
  17.8 0.6 compare_reduce_fusion
  19.2 0.6 fusion.8
  20.9 42.3 %all-to-all-done = f32[8,24,2560]{2,1,0:T(8,128)S(1)} async-done(((f32[8,24,2560]{2,1,0:T(8,128)}), f32[8,24,2560]{2,1,0:T(8,128)S(1)}, u32[]{:S(2)}, u32[]{:S(2)}) %all-to-all-start) | async-done | bytes 1966112 | tf_op jit(solution)/shard_map/all_to_all | solution.py:38
  63.2 0.1 copy.13
  63.4 21.7 %conditional.1 = (bf16[96,2560]{1,0:T(8,128)(2,1)S(1)}, bf16[96,2560]{1,0:T(8,128)(2,1)S(1)}) conditional(s32[]{:T(128)} %convert_element_type.10, () %tuple.22, f32[2,4,24,2560]{3,2,1,0:T(8,128)S(1)} %bitcast.50), branch_computations={%region_1.2_spmd, %region_2.4_spmd} | conditional | flops 5776128000 | bytes 37847088 | solution.py:52
  63.4 0.4 multiply_reduce_fusion
  63.8 0.3 bitcast_divide_fusion
  64.1 1.9 %fusion.9 = f32[2,96,96]{2,1,0:T(8,128)S(1)} fusion(f32[2,96,2560]{2,1,0:T(8,128)S(1)} %bitcast_divide_fusion), kind=kOutput, calls=%fused_computation.35 | convolution fusion | flops 566231040 | bytes 2039808 | tf_op jit(solution)/shard_map/cond/branch_1_fun/kij,klj->kil/dot_general | solution.py:24
  66.0 0.2 fusion.2
  66.2 1.9 %convolution_add_fusion.4 = f32[2,96,2560]{2,1,0:T(8,128)S(1)} fusion(f32[2,96,96]{2,1,0:T(8,128)S(1)} %fusion.2, f32[2,96,2560]{2,1,0:T(8,128)S(1)} %bitcast_divide_fusion), kind=kOutput, calls=%fused_computation.5 | convolution fusion | flops 567214080 | bytes 4005888 | tf_op jit(solution)/shard_map/cond/branch_1_fun/kij,kjl->kil/dot_general | solution.py:27
  68.2 1.9 %fusion.10 = f32[2,96,96]{2,1,0:T(8,128)S(1)} fusion(f32[2,96,2560]{2,1,0:T(8,128)S(1)} %convolution_add_fusion.4), kind=kOutput, calls=%fused_computation.36 | convolution fusion | flops 566231040 | bytes 2039808 | tf_op jit(solution)/shard_map/cond/branch_1_fun/kij,klj->kil/dot_general | solution.py:24
  70.1 0.2 fusion.3
  70.3 1.9 %convolution_add_fusion.3 = f32[2,96,2560]{2,1,0:T(8,128)S(1)} fusion(f32[2,96,96]{2,1,0:T(8,128)S(1)} %fusion.3, f32[2,96,2560]{2,1,0:T(8,128)S(1)} %convolution_add_fusion.4), kind=kOutput, calls=%fused_computation.4 | convolution fusion | flops 567214080 | bytes 4005888 | tf_op jit(solution)/shard_map/cond/branch_1_fun/kij,kjl->kil/dot_general | solution.py:27
  72.3 1.9 %fusion.11 = f32[2,96,96]{2,1,0:T(8,128)S(1)} fusion(f32[2,96,2560]{2,1,0:T(8,128)S(1)} %convolution_add_fusion.3), kind=kOutput, calls=%fused_computation.37 | convolution fusion | flops 566231040 | bytes 2039808 | tf_op jit(solution)/shard_map/cond/branch_1_fun/kij,klj->kil/dot_general | solution.py:24
  74.2 0.2 fusion.4
  74.4 1.9 %convolution_add_fusion.2 = f32[2,96,2560]{2,1,0:T(8,128)S(1)} fusion(f32[2,96,96]{2,1,0:T(8,128)S(1)} %fusion.4, f32[2,96,2560]{2,1,0:T(8,128)S(1)} %convolution_add_fusion.3), kind=kOutput, calls=%fused_computation.3 | convolution fusion | flops 567214080 | bytes 4005888 | tf_op jit(solution)/shard_map/cond/branch_1_fun/kij,kjl->kil/dot_general | solution.py:27
  76.4 2.1 %fusion.12 = f32[2,96,96]{2,1,0:T(8,128)S(1)} fusion(f32[2,96,2560]{2,1,0:T(8,128)S(1)} %convolution_add_fusion.2), kind=kOutput, calls=%fused_computation.38 | convolution fusion | flops 566231040 | bytes 2039808 | tf_op jit(solution)/shard_map/cond/branch_1_fun/kij,klj->kil/dot_general | solution.py:24
  78.4 0.2 fusion.5
  78.7 1.9 %convolution_add_fusion.1 = f32[2,96,2560]{2,1,0:T(8,128)S(1)} fusion(f32[2,96,96]{2,1,0:T(8,128)S(1)} %fusion.5, f32[2,96,2560]{2,1,0:T(8,128)S(1)} %convolution_add_fusion.2), kind=kOutput, calls=%fused_computation.2 | convolution fusion | flops 567214080 | bytes 4005888 | tf_op jit(solution)/shard_map/cond/branch_1_fun/kij,kjl->kil/dot_general | solution.py:27
  80.6 1.9 %fusion.13 = f32[2,96,96]{2,1,0:T(8,128)S(1)} fusion(f32[2,96,2560]{2,1,0:T(8,128)S(1)} %convolution_add_fusion.1), kind=kOutput, calls=%fused_computation.39 | convolution fusion | flops 566231040 | bytes 2039808 | tf_op jit(solution)/shard_map/cond/branch_1_fun/kij,klj->kil/dot_general | solution.py:24
  82.5 0.2 fusion.6
  82.8 2.0 %fusion.1 = bf16[2,96,2560]{2,1,0:T(8,128)(2,1)S(1)} fusion(f32[2,96,96]{2,1,0:T(8,128)S(1)} %fusion.6, f32[2,96,2560]{2,1,0:T(8,128)S(1)} %convolution_add_fusion.1), kind=kOutput, calls=%fused_computation.6 | convolution fusion | flops 568197120 | bytes 3022848 | tf_op jit(solution)/shard_map/cond/branch_1_fun/kij,kjl->kil/dot_general | solution.py:27
  84.8 0.1 slice_bitcast_fusion
  85.1 1.1 select_bitcast_fusion
  86.2 0.0 all-reduce.3.cloned.1.call-update
  86.2 55.7 %all-reduce.3.cloned.1.call-done = (bf16[1,96,2560]{2,1,0:T(8,128)(2,1)}, bf16[1,96,2560]{2,1,0:T(8,128)(2,1)}) async-done(((bf16[1,96,2560]{2,1,0:T(8,128)(2,1)}, bf16[1,96,2560]{2,1,0:T(8,128)(2,1)}), (bf16[1,96,2560]{2,1,0:T(8,128)(2,1)}, bf16[1,96,2560]{2,1,0:T(8,128)(2,1)})) %all-reduce.3.cloned.1.call-update) | async-done | bytes 983056 | tf_op jit(solution)/shard_map/psum | solution.py:17
  141.8 1.3 pad_maximum_fusion
  143.1 2.0 %copy.10 = bf16[2,96,2560]{2,0,1:T(2,128)(2,1)} copy(bf16[2,96,2560]{2,1,0:T(8,128)(2,1)S(1)} %pad_maximum_fusion) | data formatting | bytes 1966080 | tf_op jit(solution)/shard_map/stack | solution.py:56
  145.1 4.4 %all-to-all-start.1 = ((bf16[2,96,2560]{2,0,1:T(2,128)(2,1)}), bf16[2,96,2560]{2,0,1:T(2,128)(2,1)S(1)}, u32[]{:S(2)}, u32[]{:S(2)}) async-start(bf16[2,96,2560]{2,0,1:T(2,128)(2,1)} %copy.10), calls=%async_computation.1 | async-start | bytes 1966080 | tf_op jit(solution)/shard_map/all_to_all | solution.py:57
  149.5 23.4 %all-to-all-done.1 = bf16[2,96,2560]{2,0,1:T(2,128)(2,1)S(1)} async-done(((bf16[2,96,2560]{2,0,1:T(2,128)(2,1)}), bf16[2,96,2560]{2,0,1:T(2,128)(2,1)S(1)}, u32[]{:S(2)}, u32[]{:S(2)}) %all-to-all-start.1) | async-done | bytes 983072 | tf_op jit(solution)/shard_map/all_to_all | solution.py:57
  173.0 0.1 copy.11
  173.1 0.8 constant_dynamic-slice_fusion
  (2 shorter events, 0.0 us)
Async XLA Ops:
  11.5 51.7 %all-to-all-start = ((f32[8,24,2560]{2,1,0:T(8,128)}), f32[8,24,2560]{2,1,0:T(8,128)S(1)}, u32[]{:S(2)}, u32[]{:S(2)}) async-start(f32[8,24,2560]{2,1,0:T(8,128)} %get-tuple-element.20), calls=%async_computation | async-start | bytes 3932160 | tf_op jit(solution)/shard_map/all_to_all | solution.py:38
  17.8 124.0 %all-reduce.3.cloned.1.call-start = ((), (), s32[]{:S(2)}) async-start(), calls=%async_computation.2 | async-start | bytes 1966080 | tf_op jit(solution)/shard_map/psum | solution.py:17
  145.1 27.9 %all-to-all-start.1 = ((bf16[2,96,2560]{2,0,1:T(2,128)(2,1)}), bf16[2,96,2560]{2,0,1:T(2,128)(2,1)S(1)}, u32[]{:S(2)}, u32[]{:S(2)}) async-start(bf16[2,96,2560]{2,0,1:T(2,128)(2,1)} %copy.10), calls=%async_computation.1 | async-start | bytes 1966080 | tf_op jit(solution)/shard_map/all_to_all | solution.py:57
Sparse Core Ops, SparseCore 0:
  86.3 55.4 all-reduce.2
where the time goes:
time: 181 us
  waiting for transfers between devices  121 us (67%)
  matrix products  20.6 us (11%)
  between operations  15.9 us (9%)
  starting transfers between devices  10.8 us (6%)
  other arithmetic  8.01 us (4%)
  local copies, waits for them, and re-layouts  3.64 us (2%)
    psum x1, waiting for transfers between devices, broadcast(): return lax.psum(jnp.where(mine, x, jnp.zeros_like(x)), axis)  55.7 us
    all_to_all x1, waiting for transfers between devices, per_device(): lax.all_to_all(effective_rows, 'shard', split_axis=0, concat_axis=1, tile...  42.3 us
    all_to_all x1, waiting for transfers between devices, per_device(): lax.all_to_all(stacked, 'shard', split_axis=1, concat_axis=0, tiled=True)  23.4 us
    dot_general x5, matrix products, batched_schulz(): jnp.einsum('kij,kjl->kil', poly_mat, iterate, precision=lax.Precision.HIG...  9.76 us
    dot_general x5, matrix products, batched_schulz(): jnp.einsum('kij,klj->kil', iterate, iterate, precision=lax.Precision.HIGH...  9.67 us
    all_to_all x1, starting transfers between devices, per_device(): lax.all_to_all(effective_rows, 'shard', split_axis=0, concat_axis=1, tile...  6.32 us
    all_to_all x1, starting transfers between devices, per_device(): lax.all_to_all(stacked, 'shard', split_axis=1, concat_axis=0, tiled=True)  4.45 us
    add x1, other arithmetic, per_device(): effective_rows = gradient_values + momentum_decay * new_momentum  4.36 us
  transfers between devices with their start and end apart: 3, of which 3 were waited for; matrix products, arithmetic and copies ran while one was open for 1% of the time, Pallas kernels for 0%

commit v1 on v0

--- a/solution.py
+++ b/solution.py
@@ -10,6 +10,32 @@
 momentum_decay = 0.95
 norm_floor = 1e-07
 quintic_terms = (3.4445, -4.775, 2.0315)
+
+
+def grid_solve(content):
+    peer_axis = "shard"
+    vec_out, frame_out = (lax.axis_size(peer_axis), lax.axis_index(peer_axis))
+    near = list(content.shape)
+    earlier = content.shape[1] // vec_out
+    near[1] = earlier
+    block_last = near[0]
+    near[0] = block_last * vec_out
+    field_out = jnp.zeros(near, content.dtype)
+    num = 0
+    while num < vec_out:
+        reply = lax.dynamic_slice_in_dim(content, (frame_out ^ num) * earlier, earlier, axis=1)
+        if num:
+            xs_all = []
+            dd = 0
+            while dd < vec_out:
+                xs_all.append((dd, dd ^ num))
+                dd += 1
+            reply = lax.ppermute(reply, peer_axis, perm=xs_all)
+        field_out = lax.dynamic_update_slice_in_dim(
+            field_out, reply, (frame_out ^ num) * block_last, axis=0
+        )
+        num += 1
+    return field_out
 
 
 def broadcast(x, axis, root):
@@ -54,7 +80,7 @@
     for slot_index in range(slot_count):
         copies.append(broadcast(local_updates[slot_index], "rep", slot_owners[slot_index]))
     stacked = jnp.stack(copies)
-    result_rows = lax.all_to_all(stacked, "shard", split_axis=1, concat_axis=0, tiled=True)
+    result_rows = grid_solve(stacked)
     col_width = result_rows.shape[2] // replicas
     kept_cols = lax.dynamic_slice_in_dim(result_rows, replica * col_width, col_width, 2)
     return (kept_cols, new_momentum)

time: 181 us -> 174 us (0.961)
  waiting for transfers between devices: 121 us -> 115 us
    all_to_all x1 -> x0, waiting for transfers between devices: 23.4 us -> none  [per_device(): lax.all_to_all(stacked, 'shard', split_axis=1, concat_axis=0, tiled=True)]
    ppermute x0 -> x3, waiting for transfers between devices: none -> 17.3 us  [grid_solve(): reply = lax.ppermute(reply, peer_axis, perm=xs_all)]
    ppermute x0 -> x3, starting transfers between devices: none -> 4.45 us  [grid_solve(): reply = lax.ppermute(reply, peer_axis, perm=xs_all)]
    all_to_all x1 -> x0, starting transfers between devices: 4.45 us -> none  [per_device(): lax.all_to_all(stacked, 'shard', split_axis=1, concat_axis=0, tiled=True)]
  transfers between devices with their start and end apart: 3 -> 5, of which waited for: 3 -> 4; matrix products, arithmetic and copies ran while one was open for 1% -> 1% of each run, Pallas kernels for 0% -> 0%
where the time goes in v1:
time: 174 us
  waiting for transfers between devices  115 us (66%)
  matrix products  20.6 us (12%)
  between operations  16 us (9%)
  starting transfers between devices  10.8 us (6%)
  other arithmetic  6.76 us (4%)
  local copies, waits for them, and re-layouts  3.94 us (2%)
    psum x1, waiting for transfers between devices, broadcast(): return lax.psum(jnp.where(mine, x, jnp.zeros_like(x)), axis)  55.6 us
    all_to_all x1, waiting for transfers between devices, per_device(): lax.all_to_all(effective_rows, 'shard', split_axis=0, concat_axis=1, tile...  42.2 us
    ppermute x3, waiting for transfers between devices, grid_solve(): reply = lax.ppermute(reply, peer_axis, perm=xs_all)  17.3 us
    dot_general x5, matrix products, batched_schulz(): jnp.einsum('kij,kjl->kil', poly_mat, iterate, precision=lax.Precision.HIG...  9.76 us
    dot_general x5, matrix products, batched_schulz(): jnp.einsum('kij,klj->kil', iterate, iterate, precision=lax.Precision.HIGH...  9.67 us
    all_to_all x1, starting transfers between devices, per_device(): lax.all_to_all(effective_rows, 'shard', split_axis=0, concat_axis=1, tile...  6.32 us
    ppermute x3, starting transfers between devices, grid_solve(): reply = lax.ppermute(reply, peer_axis, perm=xs_all)  4.45 us
    add x1, other arithmetic, per_device(): effective_rows = gradient_values + momentum_decay * new_momentum  4.37 us
  transfers between devices with their start and end apart: 5, of which 4 were waited for; matrix products, arithmetic and copies ran while one was open for 1% of the time, Pallas kernels for 0%

profile of v1, /device:TPU:0, one launch (start us, length us, event | category | flops | bytes accessed | tf_op | source)
XLA Modules:
  0.0 173.6 jit_solution(2564470908109951573)
XLA Ops:
  7.2 4.4 %convert_add_fusion = (f32[8,24,2560]{2,1,0:T(8,128)}, f32[8,24,2560]{2,1,0:T(8,128)}) fusion(bf16[8,24,2560]{2,1,0:T(8,128)(2,1)} %param.4, f32[8,24,2560]{2,1,0:T(8,128)} %param.5), kind=kLoop, calls=%fused_computation.22 | loop fusion | flops 2457600 | bytes 6881280 | tf_op jit(solution)/shard_map/add | solution.py:63
  11.5 6.3 %all-to-all-start = ((f32[8,24,2560]{2,1,0:T(8,128)}), f32[8,24,2560]{2,1,0:T(8,128)S(1)}, u32[]{:S(2)}, u32[]{:S(2)}) async-start(f32[8,24,2560]{2,1,0:T(8,128)} %get-tuple-element.20), calls=%async_computation | async-start | bytes 3932160 | tf_op jit(solution)/shard_map/all_to_all | solution.py:64
  17.9 0.0 all-reduce.3.cloned.1.call-start
  17.9 0.6 compare_reduce_fusion
  19.2 0.6 fusion.8
  21.0 42.2 %all-to-all-done = f32[8,24,2560]{2,1,0:T(8,128)S(1)} async-done(((f32[8,24,2560]{2,1,0:T(8,128)}), f32[8,24,2560]{2,1,0:T(8,128)S(1)}, u32[]{:S(2)}, u32[]{:S(2)}) %all-to-all-start) | async-done | bytes 1966112 | tf_op jit(solution)/shard_map/all_to_all | solution.py:64
  63.2 0.1 copy.6
  63.4 21.7 %conditional.1 = (bf16[96,2560]{1,0:T(8,128)(2,1)S(1)}, bf16[96,2560]{1,0:T(8,128)(2,1)S(1)}) conditional(s32[]{:T(128)} %convert_element_type.10, () %tuple.22, f32[2,4,24,2560]{3,2,1,0:T(8,128)S(1)} %bitcast.46), branch_computations={%region_1.2_spmd, %region_2.4_spmd} | conditional | flops 5776128000 | bytes 37847088 | solution.py:78
  63.4 0.4 multiply_reduce_fusion
  63.8 0.3 bitcast_divide_fusion
  64.1 1.9 %fusion.9 = f32[2,96,96]{2,1,0:T(8,128)S(1)} fusion(f32[2,96,2560]{2,1,0:T(8,128)S(1)} %bitcast_divide_fusion), kind=kOutput, calls=%fused_computation.43 | convolution fusion | flops 566231040 | bytes 2039808 | tf_op jit(solution)/shard_map/cond/branch_1_fun/kij,klj->kil/dot_general | solution.py:50
  66.0 0.2 fusion.2
  66.2 1.9 %convolution_add_fusion.4 = f32[2,96,2560]{2,1,0:T(8,128)S(1)} fusion(f32[2,96,96]{2,1,0:T(8,128)S(1)} %fusion.2, f32[2,96,2560]{2,1,0:T(8,128)S(1)} %bitcast_divide_fusion), kind=kOutput, calls=%fused_computation.5 | convolution fusion | flops 567214080 | bytes 4005888 | tf_op jit(solution)/shard_map/cond/branch_1_fun/kij,kjl->kil/dot_general | solution.py:53
  68.2 1.9 %fusion.10 = f32[2,96,96]{2,1,0:T(8,128)S(1)} fusion(f32[2,96,2560]{2,1,0:T(8,128)S(1)} %convolution_add_fusion.4), kind=kOutput, calls=%fused_computation.44 | convolution fusion | flops 566231040 | bytes 2039808 | tf_op jit(solution)/shard_map/cond/branch_1_fun/kij,klj->kil/dot_general | solution.py:50
  70.1 0.2 fusion.3
  70.3 1.9 %convolution_add_fusion.3 = f32[2,96,2560]{2,1,0:T(8,128)S(1)} fusion(f32[2,96,96]{2,1,0:T(8,128)S(1)} %fusion.3, f32[2,96,2560]{2,1,0:T(8,128)S(1)} %convolution_add_fusion.4), kind=kOutput, calls=%fused_computation.4 | convolution fusion | flops 567214080 | bytes 4005888 | tf_op jit(solution)/shard_map/cond/branch_1_fun/kij,kjl->kil/dot_general | solution.py:53
  72.3 1.9 %fusion.11 = f32[2,96,96]{2,1,0:T(8,128)S(1)} fusion(f32[2,96,2560]{2,1,0:T(8,128)S(1)} %convolution_add_fusion.3), kind=kOutput, calls=%fused_computation.45 | convolution fusion | flops 566231040 | bytes 2039808 | tf_op jit(solution)/shard_map/cond/branch_1_fun/kij,klj->kil/dot_general | solution.py:50
  74.2 0.2 fusion.4
  74.4 1.9 %convolution_add_fusion.2 = f32[2,96,2560]{2,1,0:T(8,128)S(1)} fusion(f32[2,96,96]{2,1,0:T(8,128)S(1)} %fusion.4, f32[2,96,2560]{2,1,0:T(8,128)S(1)} %convolution_add_fusion.3), kind=kOutput, calls=%fused_computation.3 | convolution fusion | flops 567214080 | bytes 4005888 | tf_op jit(solution)/shard_map/cond/branch_1_fun/kij,kjl->kil/dot_general | solution.py:53
  76.4 2.1 %fusion.12 = f32[2,96,96]{2,1,0:T(8,128)S(1)} fusion(f32[2,96,2560]{2,1,0:T(8,128)S(1)} %convolution_add_fusion.2), kind=kOutput, calls=%fused_computation.46 | convolution fusion | flops 566231040 | bytes 2039808 | tf_op jit(solution)/shard_map/cond/branch_1_fun/kij,klj->kil/dot_general | solution.py:50
  78.5 0.2 fusion.5
  78.7 1.9 %convolution_add_fusion.1 = f32[2,96,2560]{2,1,0:T(8,128)S(1)} fusion(f32[2,96,96]{2,1,0:T(8,128)S(1)} %fusion.5, f32[2,96,2560]{2,1,0:T(8,128)S(1)} %convolution_add_fusion.2), kind=kOutput, calls=%fused_computation.2 | convolution fusion | flops 567214080 | bytes 4005888 | tf_op jit(solution)/shard_map/cond/branch_1_fun/kij,kjl->kil/dot_general | solution.py:53
  80.7 1.9 %fusion.13 = f32[2,96,96]{2,1,0:T(8,128)S(1)} fusion(f32[2,96,2560]{2,1,0:T(8,128)S(1)} %convolution_add_fusion.1), kind=kOutput, calls=%fused_computation.47 | convolution fusion | flops 566231040 | bytes 2039808 | tf_op jit(solution)/shard_map/cond/branch_1_fun/kij,klj->kil/dot_general | solution.py:50
  82.6 0.2 fusion.6
  82.8 2.0 %fusion.1 = bf16[2,96,2560]{2,1,0:T(8,128)(2,1)S(1)} fusion(f32[2,96,96]{2,1,0:T(8,128)S(1)} %fusion.6, f32[2,96,2560]{2,1,0:T(8,128)S(1)} %convolution_add_fusion.1), kind=kOutput, calls=%fused_computation.6 | convolution fusion | flops 568197120 | bytes 3022848 | tf_op jit(solution)/shard_map/cond/branch_1_fun/kij,kjl->kil/dot_general | solution.py:53
  84.8 0.1 slice_bitcast_fusion
  85.1 1.1 select_bitcast_fusion
  86.2 0.0 all-reduce.3.cloned.1.call-update
  86.2 55.6 %all-reduce.3.cloned.1.call-done = (bf16[1,96,2560]{2,1,0:T(8,128)(2,1)}, bf16[1,96,2560]{2,1,0:T(8,128)(2,1)}) async-done(((bf16[1,96,2560]{2,1,0:T(8,128)(2,1)}, bf16[1,96,2560]{2,1,0:T(8,128)(2,1)}), (bf16[1,96,2560]{2,1,0:T(8,128)(2,1)}, bf16[1,96,2560]{2,1,0:T(8,128)(2,1)})) %all-reduce.3.cloned.1.call-update) | async-done | bytes 983056 | tf_op jit(solution)/shard_map/psum | solution.py:43
  141.9 1.1 constant_dynamic-update-slice_fusion.1
  142.9 1.1 constant_dynamic-update-slice_fusion
  144.0 0.1 broadcast_in_dim.4
  144.1 0.1 constant_dynamic-slice_fusion
  144.2 1.4 collective-permute-start
  145.6 2.4 %collective-permute-start.1 = (bf16[2,24,2560]{2,1,0:T(8,128)(2,1)S(1)}, bf16[2,24,2560]{2,1,0:T(8,128)(2,1)S(1)}, u32[]{:S(2)}, u32[]{:S(2)}) collective-permute-start(bf16[2,24,2560]{2,1,0:T(8,128)(2,1)S(1)} %get-tuple-element.25), channel_id=1, source_target_pairs={{0,2},{1,3},{2,0},{3,1},{4,6},{5,7},{6,4},{7,5},{8,10},{9,11},{10,... | collective-permute-start | bytes 737288 | tf_op jit(solution)/shard_map/ppermute | solution.py:33
  148.0 0.6 collective-permute-start.2
  148.6 6.2 %collective-permute-done = bf16[2,24,2560]{2,1,0:T(8,128)(2,1)S(1)} collective-permute-done((bf16[2,24,2560]{2,1,0:T(8,128)(2,1)S(1)}, bf16[2,24,2560]{2,1,0:T(8,128)(2,1)S(1)}, u32[]{:S(2)}, u32[]{:S(2)}) %collective-permute-start) | collective-permute-done | bytes 245792 | tf_op jit(solution)/shard_map/ppermute | solution.py:33
  154.9 11.0 %collective-permute-done.1 = bf16[2,24,2560]{2,1,0:T(8,128)(2,1)S(1)} collective-permute-done((bf16[2,24,2560]{2,1,0:T(8,128)(2,1)S(1)}, bf16[2,24,2560]{2,1,0:T(8,128)(2,1)S(1)}, u32[]{:S(2)}, u32[]{:S(2)}) %collective-permute-start.1) | collective-permute-done | bytes 245792 | tf_op jit(solution)/shard_map/ppermute | solution.py:33
  165.9 0.0 collective-permute-done.2
  166.0 0.8 constant_dynamic-slice_fusion.3
  (5 shorter events, 0.1 us)
Async XLA Ops:
  11.5 51.7 %all-to-all-start = ((f32[8,24,2560]{2,1,0:T(8,128)}), f32[8,24,2560]{2,1,0:T(8,128)S(1)}, u32[]{:S(2)}, u32[]{:S(2)}) async-start(f32[8,24,2560]{2,1,0:T(8,128)} %get-tuple-element.20), calls=%async_computation | async-start | bytes 3932160 | tf_op jit(solution)/shard_map/all_to_all | solution.py:64
  17.9 124.0 %all-reduce.3.cloned.1.call-start = ((), (), s32[]{:S(2)}) async-start(), calls=%async_computation.1 | async-start | bytes 1966080 | tf_op jit(solution)/shard_map/psum | solution.py:43
  144.2 10.7 %collective-permute-start = (bf16[2,24,2560]{2,1,0:T(8,128)(2,1)S(1)}, bf16[2,24,2560]{2,1,0:T(8,128)(2,1)S(1)}, u32[]{:S(2)}, u32[]{:S(2)}) collective-permute-start(bf16[2,24,2560]{2,1,0:T(8,128)(2,1)S(1)} %get-tuple-element.26), channel_id=1, source_target_pairs={{0,1},{1,0},{2,3},{3,2},{4,5},{5,4},{6,7},{7,6},{8,9},{9,8},{10,11... | collective-permute-start | bytes 737288 | tf_op jit(solution)/shard_map/ppermute | solution.py:33
  145.6 20.3 %collective-permute-start.1 = (bf16[2,24,2560]{2,1,0:T(8,128)(2,1)S(1)}, bf16[2,24,2560]{2,1,0:T(8,128)(2,1)S(1)}, u32[]{:S(2)}, u32[]{:S(2)}) collective-permute-start(bf16[2,24,2560]{2,1,0:T(8,128)(2,1)S(1)} %get-tuple-element.25), channel_id=1, source_target_pairs={{0,2},{1,3},{2,0},{3,1},{4,6},{5,7},{6,4},{7,5},{8,10},{9,11},{10,... | collective-permute-start | bytes 737288 | tf_op jit(solution)/shard_map/ppermute | solution.py:33
  148.0 17.9 %collective-permute-start.2 = (bf16[2,24,2560]{2,1,0:T(8,128)(2,1)S(1)}, bf16[2,24,2560]{2,1,0:T(8,128)(2,1)S(1)}, u32[]{:S(2)}, u32[]{:S(2)}) collective-permute-start(bf16[2,24,2560]{2,1,0:T(8,128)(2,1)S(1)} %get-tuple-element.24), channel_id=1, source_target_pairs={{0,3},{1,2},{2,1},{3,0},{4,7},{5,6},{6,5},{7,4},{8,11},{9,10},{10,... | collective-permute-start | bytes 737288 | tf_op jit(solution)/shard_map/ppermute | solution.py:33
Sparse Core Ops, SparseCore 0:
  86.3 55.4 all-reduce.2
